TPU v7x, 32 devices: a whole 2x2x4 slice. The times are simulated.
32 devices in a mesh: section: 8 (over z, x), fsdp: 4 (over y, core).
Axes of the slice: x: 2, y: 2, z: 4, core: 2. Of those that a mesh axis runs over, the one named last changes fastest.
Arguments:
- acts: bfloat16 [8, 2304, 2048], P('section', 'fsdp'), may hold values from -6 to 6
- gains: float32 [8, 2048], P('section'), may hold values from 0.5 to 1.5
- proj: bfloat16 [8, 2048, 2048], P('section', 'fsdp'), may hold values from -0.0625 to 0.0625
- head: bfloat16 [2048, 512], replicated, may hold values from -1 to 1
- segs: int32 [12, 192], P('fsdp'), may hold values from 0 to 15, never falling along the last dimension, each value on 1 to 24 neighbouring positions
- labels: int32 [12, 16], P('fsdp'), may hold values from 0 to 511
Outputs:
- din: bfloat16 [8, 2304, 2048], P('section', 'fsdp')
- dproj: bfloat16 [8, 2048, 2048], P('section', 'fsdp')
- dgain: float32 [8, 2048], P('section')
Inputs may be any that keep to these rules, and one draw needn't show every extreme that they name: `segs`: each row lists the candidates of one microbatch in order, every candidate has at least one token and one has 24.
All inputs are finite; a program needn't handle non-finite values.
Results may differ from a plain program's by a relative error of at most 0.04.
Values may be sent and summed in bfloat16 or wider, within the bound.
A program may use at most 128 MiB of HBM per device.

v0:
```python
import jax
import jax.numpy as jnp
from jax import lax
from jax.sharding import PartitionSpec as P

norm_eps = 1e-06


def from_behind(value, axis, by):
    length = lax.axis_size(axis)
    pairs = [(i, i + by) for i in range(length) if 0 <= i + by < length]
    return lax.ppermute(value, axis, pairs)


def per_device(acts, gains, proj, head, segs, labels):
    layer_in = acts[0]
    gain = gains[0]
    sections = lax.axis_size("section")
    section_pos = lax.axis_index("section")
    batches, rows = segs.shape
    width = layer_in.shape[1]
    cands = labels.shape[1]
    classes = head.shape[1]
    weight = lax.all_gather(proj[0], "fsdp", axis=0, tiled=True)
    x_float = layer_in.astype(jnp.float32)
    inv_rms = lax.rsqrt(jnp.mean(x_float * x_float, -1, keepdims=True) + norm_eps)
    x_hat = x_float * inv_rms
    normed = (x_hat * gain).astype(jnp.bfloat16)
    onehot = (segs[:, None, :] == jnp.arange(cands, dtype=jnp.int32)[None, :, None]).astype(
        jnp.float32
    )
    counts = jnp.sum(onehot, -1)

    def top_grad(unused):
        y_top = x_float + jnp.dot(normed, weight, preferred_element_type=jnp.float32)
        y_blocks = y_top.reshape(batches, rows, width)
        pooled = (jnp.einsum("mcr,mrd->mcd", onehot, y_blocks) / counts[..., None]).astype(
            jnp.bfloat16
        )
        logits = jnp.dot(pooled.reshape(-1, width), head, preferred_element_type=jnp.float32)
        target = (
            labels.reshape(-1)[:, None] == jnp.arange(classes, dtype=jnp.int32)[None, :]
        ).astype(jnp.float32)
        dlogit = (jax.nn.sigmoid(logits) - target).astype(jnp.bfloat16)
        dpool = jnp.dot(dlogit, head.T, preferred_element_type=jnp.float32).reshape(
            batches, cands, width
        )
        dpool = dpool / counts[..., None]
        return jnp.einsum("mcr,mcd->mrd", onehot, dpool).astype(jnp.bfloat16)

    def no_grad(unused):
        return jnp.zeros((batches, rows, width), jnp.bfloat16)

    top_grads = lax.cond(section_pos == sections - 1, top_grad, no_grad, 0)
    hat_blocks = x_hat.reshape(batches, rows, width)
    rms_blocks = inv_rms.reshape(batches, rows, 1)

    def backward_one(carry, mb_index, grad_in):
        grads, din, gain_acc, acc, sent = carry
        hat_piece = lax.dynamic_index_in_dim(hat_blocks, mb_index, 0, False)
        rms_piece = lax.dynamic_index_in_dim(rms_blocks, mb_index, 0, False)
        back = lax.dot_general(
            grad_in, weight, (((1,), (1,)), ((), ())), preferred_element_type=jnp.float32
        )
        scaled = back * gain
        through = rms_piece * (scaled - hat_piece * jnp.mean(scaled * hat_piece, -1, keepdims=True))
        layer_grad = (grad_in.astype(jnp.float32) + through).astype(jnp.bfloat16)
        grads = lax.dynamic_update_index_in_dim(grads, grad_in, mb_index, 0)
        din = lax.dynamic_update_index_in_dim(din, layer_grad, mb_index, 0)
        gain_acc = gain_acc + jnp.sum(back * hat_piece, 0)
        return (grads, din, gain_acc, acc, layer_grad)

    def chain_step(step, carry):
        incoming = from_behind(carry[4], "section", -1)
        mbatch = step - (sections - 1 - section_pos)
        active = (mbatch >= 0) & (mbatch < batches)
        mb_index = jnp.clip(mbatch, 0, batches - 1)
        own_top = lax.dynamic_index_in_dim(top_grads, mb_index, 0, False)
        grad_in = jnp.where(section_pos == sections - 1, own_top, incoming)

        def waiting(state):
            return state

        return lax.cond(
            active, lambda state: backward_one(state, mb_index, grad_in), waiting, carry
        )

    acc_shape = (1, 1)
    start = (
        jnp.zeros((batches, rows, width), jnp.bfloat16),
        jnp.zeros((batches, rows, width), jnp.bfloat16),
        jnp.zeros((width,), jnp.float32),
        jnp.zeros(acc_shape, jnp.float32),
        jnp.zeros((rows, width), jnp.bfloat16),
    )
    grads, din, gain_acc, acc, sent = lax.fori_loop(0, sections + batches - 1, chain_step, start)
    gain_total = lax.psum(gain_acc, "fsdp")
    flat_grads = grads.reshape(-1, width)
    weight_part = lax.psum_scatter(
        lax.dot_general(
            normed, flat_grads, (((0,), (0,)), ((), ())), preferred_element_type=jnp.float32
        ).astype(jnp.bfloat16),
        "fsdp",
        scatter_dimension=0,
        tiled=True,
    )
    return (din.reshape(1, -1, width), weight_part[None], gain_total[None])


def solution(mesh):
    return jax.shard_map(
        per_device,
        mesh=mesh,
        in_specs=(
            P("section", "fsdp", None),
            P("section", None),
            P("section", "fsdp", None),
            P(),
            P("fsdp", None),
            P("fsdp", None),
        ),
        out_specs=(P("section", "fsdp", None), P("section", "fsdp", None), P("section", None)),
        check_vma=False,
    )
```

profile of v0, /device:TPU:0, one launch (start us, length us, event | category | flops | bytes accessed | tf_op | source)
XLA Modules:
  0.0 488.1 jit_solution(12886816777150107079)
XLA Ops:
  7.2 0.0 copy-start
  7.2 0.0 copy-start.2
  7.2 0.0 copy-start.1
  7.2 0.0 all-gather.3.cloned.1.call-start
  7.2 0.7 all-gather.3.cloned.1.call-update
  7.9 0.0 reduce-scatter.2.cloned.1.call-start
  8.0 2.2 multiply_reduce_fusion
  10.2 0.1 rsqrt.23
  10.3 0.1 rsqrt.24
  10.4 0.0 copy-done.2
  10.4 0.0 copy-done
  10.4 0.0 copy-done.1
  10.4 2.0 multiply_convert_fusion.1
  12.4 2.7 convert_bitcast_fusion
  15.1 0.0 copy-start.3
  15.1 2.5 broadcast_multiply_fusion.1
  17.7 53.0 %all-gather.3.cloned.1.call-done = bf16[1,2048,2048]{2,1,0:T(8,128)(2,1)} async-done(((bf16[1,512,2048]{2,1,0:T(8,128)(2,1)}), bf16[1,2048,2048]{2,1,0:T(8,128)(2,1)}) %all-gather.3.cloned.1.call-update) | async-done | bytes 8388624 | tf_op jit(solution)/shard_map/all_gather | solution.py:24
  70.7 0.0 copy-done.3
  70.7 1.7 conditional.2
  70.7 1.7 broadcast.64
  72.4 1.7 broadcast.68
  74.0 1.7 broadcast.68.clone
  75.7 1.0 broadcast_in_dim.33
  76.7 325.5 %while.21 = (s32[]{:T(128)}, bf16[3,192,2048]{2,1,0:T(8,128)(2,1)}, bf16[3,192,2048]{2,1,0:T(8,128)(2,1)}, f32[2048]{0:T(1024)S(1)}, bf16[192,2048]{1,0:T(8,128)...) while((s32[]{:T(128)}, bf16[3,192,2048]{2,1,0:T(8,128)(2,1)}, ...), condition=%wide.region_9.10_spmd, body=%wide.region_4.9_spmd.sunk | while | flops 1615724544 | bytes 24172716 | solution.py:96
  76.7 1.3 collective-permute-start
  78.0 20.5 %collective-permute-done = bf16[192,2048]{1,0:T(8,128)(2,1)S(1)} collective-permute-done((bf16[192,2048]{1,0:T(8,128)(2,1)}, bf16[192,2048]{1,0:T(8,128)(2,1)S(1)}, u32[]{:S(2)}, u32[]{:S(2)}) %collective-permute-start) | collective-permute-done | bytes 786464 | tf_op jit(solution)/shard_map/while/body/eval_jaxpr/ppermute | solution.py:12
  98.5 1.3 collective-permute-start
  99.8 20.3 %collective-permute-done = bf16[192,2048]{1,0:T(8,128)(2,1)S(1)} collective-permute-done((bf16[192,2048]{1,0:T(8,128)(2,1)}, bf16[192,2048]{1,0:T(8,128)(2,1)S(1)}, u32[]{:S(2)}, u32[]{:S(2)}) %collective-permute-start) | collective-permute-done | bytes 786464 | tf_op jit(solution)/shard_map/while/body/eval_jaxpr/ppermute | solution.py:12
  120.1 1.3 collective-permute-start
  121.4 19.7 %collective-permute-done = bf16[192,2048]{1,0:T(8,128)(2,1)S(1)} collective-permute-done((bf16[192,2048]{1,0:T(8,128)(2,1)}, bf16[192,2048]{1,0:T(8,128)(2,1)S(1)}, u32[]{:S(2)}, u32[]{:S(2)}) %collective-permute-start) | collective-permute-done | bytes 786464 | tf_op jit(solution)/shard_map/while/body/eval_jaxpr/ppermute | solution.py:12
  141.1 1.3 collective-permute-start
  142.4 18.7 %collective-permute-done = bf16[192,2048]{1,0:T(8,128)(2,1)S(1)} collective-permute-done((bf16[192,2048]{1,0:T(8,128)(2,1)}, bf16[192,2048]{1,0:T(8,128)(2,1)S(1)}, u32[]{:S(2)}, u32[]{:S(2)}) %collective-permute-start) | collective-permute-done | bytes 786464 | tf_op jit(solution)/shard_map/while/body/eval_jaxpr/ppermute | solution.py:12
  161.1 1.3 collective-permute-start
  162.4 17.8 %collective-permute-done = bf16[192,2048]{1,0:T(8,128)(2,1)S(1)} collective-permute-done((bf16[192,2048]{1,0:T(8,128)(2,1)}, bf16[192,2048]{1,0:T(8,128)(2,1)S(1)}, u32[]{:S(2)}, u32[]{:S(2)}) %collective-permute-start) | collective-permute-done | bytes 786464 | tf_op jit(solution)/shard_map/while/body/eval_jaxpr/ppermute | solution.py:12
  180.2 1.3 collective-permute-start
  181.5 16.9 %collective-permute-done = bf16[192,2048]{1,0:T(8,128)(2,1)S(1)} collective-permute-done((bf16[192,2048]{1,0:T(8,128)(2,1)}, bf16[192,2048]{1,0:T(8,128)(2,1)S(1)}, u32[]{:S(2)}, u32[]{:S(2)}) %collective-permute-start) | collective-permute-done | bytes 786464 | tf_op jit(solution)/shard_map/while/body/eval_jaxpr/ppermute | solution.py:12
  198.4 1.3 collective-permute-start
  199.7 30.9 %collective-permute-done = bf16[192,2048]{1,0:T(8,128)(2,1)S(1)} collective-permute-done((bf16[192,2048]{1,0:T(8,128)(2,1)}, bf16[192,2048]{1,0:T(8,128)(2,1)S(1)}, u32[]{:S(2)}, u32[]{:S(2)}) %collective-permute-start) | collective-permute-done | bytes 786464 | tf_op jit(solution)/shard_map/while/body/eval_jaxpr/ppermute | solution.py:12
  230.7 1.3 collective-permute-start
  232.0 99.4 %collective-permute-done = bf16[192,2048]{1,0:T(8,128)(2,1)S(1)} collective-permute-done((bf16[192,2048]{1,0:T(8,128)(2,1)}, bf16[192,2048]{1,0:T(8,128)(2,1)S(1)}, u32[]{:S(2)}, u32[]{:S(2)}) %collective-permute-start) | collective-permute-done | bytes 786464 | tf_op jit(solution)/shard_map/while/body/eval_jaxpr/ppermute | solution.py:12
  331.4 12.3 %conditional.4 = ((bf16[3,192,2048]{2,1,0:T(8,128)(2,1)}, bf16[3,192,2048]{2,1,0:T(8,128)(2,1)}, f32[2048]{0:T(1024)S(1)}, bf16[192,2048]{1,0:T(8,128)(2,1)})) conditional(s32[]{:T(128)} %convert_element_type.116, (bf16[3,192,2048]{2,1,0:T(8,128)(2,1)}, bf16[3,192,2048]{2,1,0:T(8,128)(2,1)}, f32[2048]{0:T(1024)S(1)}, ...), branch_computations={%region_5.5_spmd, %region_6.8_spmd} | conditional | flops 1615724544 | bytes 21026640 | solution.py:84
  331.4 2.4 bitcast_dynamic-update-slice_fusion.1
  333.8 6.8 %fusion.19 = (f32[2048]{0:T(1024)S(1)}, f32[192]{0:T(256)S(1)}, f32[192,2048]{1,0:T(8,128)S(1)}) fusion(f32[3,192,2048]{2,1,0:T(8,128)} %get-tuple-element.405, s32[]{:T(128)S(6)} %min.11, f32[2048]{0:T(1024)S(1)} %bitcast.67, bf16[192,2048]{1,0:T(8,128)(2,1)S(1)} %get-tuple-element.466, bf16[2048,2048]{1,0:T(8,128)(2,1)} %get-tuple-element.403), kind=kOutput, calls=%fused_computation.27 | convolution fusion | flops 1612576512 | bytes 12337924 | tf_op jit(solution)/shard_map/while/body/eval_jaxpr/cond/branch_1_fun/dot_general | solution.py:62
  340.7 3.0 bitcast_dynamic-update-slice_fusion
  343.7 1.3 collective-permute-start
  345.0 16.2 %collective-permute-done = bf16[192,2048]{1,0:T(8,128)(2,1)S(1)} collective-permute-done((bf16[192,2048]{1,0:T(8,128)(2,1)}, bf16[192,2048]{1,0:T(8,128)(2,1)S(1)}, u32[]{:S(2)}, u32[]{:S(2)}) %collective-permute-start) | collective-permute-done | bytes 786464 | tf_op jit(solution)/shard_map/while/body/eval_jaxpr/ppermute | solution.py:12
  361.2 12.2 %conditional.4 = ((bf16[3,192,2048]{2,1,0:T(8,128)(2,1)}, bf16[3,192,2048]{2,1,0:T(8,128)(2,1)}, f32[2048]{0:T(1024)S(1)}, bf16[192,2048]{1,0:T(8,128)(2,1)})) conditional(s32[]{:T(128)} %convert_element_type.116, (bf16[3,192,2048]{2,1,0:T(8,128)(2,1)}, bf16[3,192,2048]{2,1,0:T(8,128)(2,1)}, f32[2048]{0:T(1024)S(1)}, ...), branch_computations={%region_5.5_spmd, %region_6.8_spmd} | conditional | flops 1615724544 | bytes 21026640 | solution.py:84
  361.2 2.3 bitcast_dynamic-update-slice_fusion.1
  363.5 6.8 %fusion.19 = (f32[2048]{0:T(1024)S(1)}, f32[192]{0:T(256)S(1)}, f32[192,2048]{1,0:T(8,128)S(1)}) fusion(f32[3,192,2048]{2,1,0:T(8,128)} %get-tuple-element.405, s32[]{:T(128)S(6)} %min.11, f32[2048]{0:T(1024)S(1)} %bitcast.67, bf16[192,2048]{1,0:T(8,128)(2,1)S(1)} %get-tuple-element.466, bf16[2048,2048]{1,0:T(8,128)(2,1)} %get-tuple-element.403), kind=kOutput, calls=%fused_computation.27 | convolution fusion | flops 1612576512 | bytes 12337924 | tf_op jit(solution)/shard_map/while/body/eval_jaxpr/cond/branch_1_fun/dot_general | solution.py:62
  370.4 3.0 bitcast_dynamic-update-slice_fusion
  373.4 1.3 collective-permute-start
  374.7 15.3 %collective-permute-done = bf16[192,2048]{1,0:T(8,128)(2,1)S(1)} collective-permute-done((bf16[192,2048]{1,0:T(8,128)(2,1)}, bf16[192,2048]{1,0:T(8,128)(2,1)S(1)}, u32[]{:S(2)}, u32[]{:S(2)}) %collective-permute-start) | collective-permute-done | bytes 786464 | tf_op jit(solution)/shard_map/while/body/eval_jaxpr/ppermute | solution.py:12
  390.0 12.2 %conditional.4 = ((bf16[3,192,2048]{2,1,0:T(8,128)(2,1)}, bf16[3,192,2048]{2,1,0:T(8,128)(2,1)}, f32[2048]{0:T(1024)S(1)}, bf16[192,2048]{1,0:T(8,128)(2,1)})) conditional(s32[]{:T(128)} %convert_element_type.116, (bf16[3,192,2048]{2,1,0:T(8,128)(2,1)}, bf16[3,192,2048]{2,1,0:T(8,128)(2,1)}, f32[2048]{0:T(1024)S(1)}, ...), branch_computations={%region_5.5_spmd, %region_6.8_spmd} | conditional | flops 1615724544 | bytes 21026640 | solution.py:84
  390.0 2.3 bitcast_dynamic-update-slice_fusion.1
  392.3 6.8 %fusion.19 = (f32[2048]{0:T(1024)S(1)}, f32[192]{0:T(256)S(1)}, f32[192,2048]{1,0:T(8,128)S(1)}) fusion(f32[3,192,2048]{2,1,0:T(8,128)} %get-tuple-element.405, s32[]{:T(128)S(6)} %min.11, f32[2048]{0:T(1024)S(1)} %bitcast.67, bf16[192,2048]{1,0:T(8,128)(2,1)S(1)} %get-tuple-element.466, bf16[2048,2048]{1,0:T(8,128)(2,1)} %get-tuple-element.403), kind=kOutput, calls=%fused_computation.27 | convolution fusion | flops 1612576512 | bytes 12337924 | tf_op jit(solution)/shard_map/while/body/eval_jaxpr/cond/branch_1_fun/dot_general | solution.py:62
  399.2 3.0 bitcast_dynamic-update-slice_fusion
  402.2 10.8 %convolution_convert_fusion.1 = bf16[2048,2048]{1,0:T(8,128)(2,1)} fusion(bf16[576,2048]{1,0:T(8,128)(2,1)} %bitcast.62, bf16[1,576,2048]{2,1,0:T(8,128)(2,1)S(1)} %copy-done, f32[2048]{0:T(1024)S(1)} %bitcast.69, f32[576]{0:T(1024)S(1)} %add_rsqrt_fusion), kind=kOutput, calls=%fused_computation.33 | convolution fusion | flops 4840751104 | bytes 13117696 | tf_op jit(solution)/shard_map/dot_general | solution.py:100
  413.0 0.0 reduce-scatter.2.cloned.1.call-update
  413.1 6.7 %psum.7 = f32[1,2048]{1,0:T(1,128)} all-reduce(f32[1,2048]{1,0:T(1,128)S(1)} %bitcast.65), channel_id=1, replica_groups=mesh['section'=8,'fsdp'=4] {'fsdp'}, use_global_device_ids=true, to_apply=%region_11.12 | all-reduce | flops 2048 | bytes 16384 | tf_op jit(solution)/shard_map/psum | solution.py:97
  419.7 61.5 %reduce-scatter.2.cloned.1.call-done = bf16[512,2048]{1,0:T(8,128)(2,1)} async-done(((bf16[2048,2048]{1,0:T(8,128)(2,1)}), bf16[512,2048]{1,0:T(8,128)(2,1)}) %reduce-scatter.2.cloned.1.call-update) | async-done | bytes 2097168 | tf_op jit(solution)/shard_map/reduce_scatter | solution.py:99
  (19 shorter events, 0.1 us)
Async XLA Ops:
  7.2 3.2 copy-start
  7.2 3.2 copy-start.2
  7.2 3.2 copy-start.1
  7.2 63.5 %all-gather.3.cloned.1.call-start = ((), (), s32[]{:S(2)}) async-start(), calls=%async_computation.2 | async-start | bytes 10485760 | tf_op jit(solution)/shard_map/all_gather | solution.py:24
  7.9 473.4 %reduce-scatter.2.cloned.1.call-start = ((), (), s32[]{:S(2)}) async-start(), calls=%async_computation.1 | async-start | bytes 10485760 | tf_op jit(solution)/shard_map/reduce_scatter | solution.py:99
  15.1 55.5 %copy-start.3 = (s32[3,16]{1,0:T(4,128)S(1)}, s32[3,16]{1,0:T(4,128)}, u32[]{:S(2)}) copy-start(s32[3,16]{1,0:T(4,128)} %param.17) | copy-start | bytes 580
  76.7 21.8 %collective-permute-start = (bf16[192,2048]{1,0:T(8,128)(2,1)}, bf16[192,2048]{1,0:T(8,128)(2,1)S(1)}, u32[]{:S(2)}, u32[]{:S(2)}) collective-permute-start(bf16[192,2048]{1,0:T(8,128)(2,1)} %get-tuple-element.576), channel_id=1, source_target_pairs={{4,0},{8,4},{12,8},{16,12},{20,16},{24,20},{28,24},{5,1},{9,5},{13... | collective-permute-start | bytes 2359304 | tf_op jit(solution)/shard_map/while/body/eval_jaxpr/ppermute | solution.py:12
  98.5 21.6 %collective-permute-start = (bf16[192,2048]{1,0:T(8,128)(2,1)}, bf16[192,2048]{1,0:T(8,128)(2,1)S(1)}, u32[]{:S(2)}, u32[]{:S(2)}) collective-permute-start(bf16[192,2048]{1,0:T(8,128)(2,1)} %get-tuple-element.576), channel_id=1, source_target_pairs={{4,0},{8,4},{12,8},{16,12},{20,16},{24,20},{28,24},{5,1},{9,5},{13... | collective-permute-start | bytes 2359304 | tf_op jit(solution)/shard_map/while/body/eval_jaxpr/ppermute | solution.py:12
  120.1 21.0 %collective-permute-start = (bf16[192,2048]{1,0:T(8,128)(2,1)}, bf16[192,2048]{1,0:T(8,128)(2,1)S(1)}, u32[]{:S(2)}, u32[]{:S(2)}) collective-permute-start(bf16[192,2048]{1,0:T(8,128)(2,1)} %get-tuple-element.576), channel_id=1, source_target_pairs={{4,0},{8,4},{12,8},{16,12},{20,16},{24,20},{28,24},{5,1},{9,5},{13... | collective-permute-start | bytes 2359304 | tf_op jit(solution)/shard_map/while/body/eval_jaxpr/ppermute | solution.py:12
  141.1 20.0 %collective-permute-start = (bf16[192,2048]{1,0:T(8,128)(2,1)}, bf16[192,2048]{1,0:T(8,128)(2,1)S(1)}, u32[]{:S(2)}, u32[]{:S(2)}) collective-permute-start(bf16[192,2048]{1,0:T(8,128)(2,1)} %get-tuple-element.576), channel_id=1, source_target_pairs={{4,0},{8,4},{12,8},{16,12},{20,16},{24,20},{28,24},{5,1},{9,5},{13... | collective-permute-start | bytes 2359304 | tf_op jit(solution)/shard_map/while/body/eval_jaxpr/ppermute | solution.py:12
  161.1 19.1 %collective-permute-start = (bf16[192,2048]{1,0:T(8,128)(2,1)}, bf16[192,2048]{1,0:T(8,128)(2,1)S(1)}, u32[]{:S(2)}, u32[]{:S(2)}) collective-permute-start(bf16[192,2048]{1,0:T(8,128)(2,1)} %get-tuple-element.576), channel_id=1, source_target_pairs={{4,0},{8,4},{12,8},{16,12},{20,16},{24,20},{28,24},{5,1},{9,5},{13... | collective-permute-start | bytes 2359304 | tf_op jit(solution)/shard_map/while/body/eval_jaxpr/ppermute | solution.py:12
  180.2 18.2 %collective-permute-start = (bf16[192,2048]{1,0:T(8,128)(2,1)}, bf16[192,2048]{1,0:T(8,128)(2,1)S(1)}, u32[]{:S(2)}, u32[]{:S(2)}) collective-permute-start(bf16[192,2048]{1,0:T(8,128)(2,1)} %get-tuple-element.576), channel_id=1, source_target_pairs={{4,0},{8,4},{12,8},{16,12},{20,16},{24,20},{28,24},{5,1},{9,5},{13... | collective-permute-start | bytes 2359304 | tf_op jit(solution)/shard_map/while/body/eval_jaxpr/ppermute | solution.py:12
  198.4 32.2 %collective-permute-start = (bf16[192,2048]{1,0:T(8,128)(2,1)}, bf16[192,2048]{1,0:T(8,128)(2,1)S(1)}, u32[]{:S(2)}, u32[]{:S(2)}) collective-permute-start(bf16[192,2048]{1,0:T(8,128)(2,1)} %get-tuple-element.576), channel_id=1, source_target_pairs={{4,0},{8,4},{12,8},{16,12},{20,16},{24,20},{28,24},{5,1},{9,5},{13... | collective-permute-start | bytes 2359304 | tf_op jit(solution)/shard_map/while/body/eval_jaxpr/ppermute | solution.py:12
  230.7 100.7 %collective-permute-start = (bf16[192,2048]{1,0:T(8,128)(2,1)}, bf16[192,2048]{1,0:T(8,128)(2,1)S(1)}, u32[]{:S(2)}, u32[]{:S(2)}) collective-permute-start(bf16[192,2048]{1,0:T(8,128)(2,1)} %get-tuple-element.576), channel_id=1, source_target_pairs={{4,0},{8,4},{12,8},{16,12},{20,16},{24,20},{28,24},{5,1},{9,5},{13... | collective-permute-start | bytes 2359304 | tf_op jit(solution)/shard_map/while/body/eval_jaxpr/ppermute | solution.py:12
  343.7 17.5 %collective-permute-start = (bf16[192,2048]{1,0:T(8,128)(2,1)}, bf16[192,2048]{1,0:T(8,128)(2,1)S(1)}, u32[]{:S(2)}, u32[]{:S(2)}) collective-permute-start(bf16[192,2048]{1,0:T(8,128)(2,1)} %get-tuple-element.576), channel_id=1, source_target_pairs={{4,0},{8,4},{12,8},{16,12},{20,16},{24,20},{28,24},{5,1},{9,5},{13... | collective-permute-start | bytes 2359304 | tf_op jit(solution)/shard_map/while/body/eval_jaxpr/ppermute | solution.py:12
  373.4 16.6 %collective-permute-start = (bf16[192,2048]{1,0:T(8,128)(2,1)}, bf16[192,2048]{1,0:T(8,128)(2,1)S(1)}, u32[]{:S(2)}, u32[]{:S(2)}) collective-permute-start(bf16[192,2048]{1,0:T(8,128)(2,1)} %get-tuple-element.576), channel_id=1, source_target_pairs={{4,0},{8,4},{12,8},{16,12},{20,16},{24,20},{28,24},{5,1},{9,5},{13... | collective-permute-start | bytes 2359304 | tf_op jit(solution)/shard_map/while/body/eval_jaxpr/ppermute | solution.py:12
Sparse Core Ops, SparseCore 0:
  9.6 61.0 all-gather.2
  413.2 68.0 reduce-scatter.1
where the time goes:
time: 489 us; the launch traced here: 488 us
  waiting for transfers between devices  391 us (80%)
  matrix products  31.3 us (6%)
  other arithmetic  25.6 us (5%)
  between operations  14.1 us (3%)
  starting transfers between devices  12.9 us (3%)
  blocking collectives  6.67 us (1%)
  local copies, waits for them, and re-layouts  6.23 us (1%)
    ppermute x10, waiting for transfers between devices, from_behind(): return lax.ppermute(value, axis, pairs)  276 us
    reduce_scatter x1, waiting for transfers between devices, per_device(): lax.psum_scatter(lax.dot_general(normed, flat_grads, (((0,), (0,)), ((),...  61.5 us
    all_gather x1, waiting for transfers between devices, per_device(): weight = lax.all_gather(proj[0], 'fsdp', axis=0, tiled=True)  53 us
    dot_general x3, matrix products, backward_one(): lax.dot_general(grad_in, weight, (((1,), (1,)), ((), ())), preferred_elem...  20.5 us
    ppermute x10, starting transfers between devices, from_behind(): return lax.ppermute(value, axis, pairs)  12.8 us
    dot_general x1, matrix products, per_device(): lax.dot_general(normed, flat_grads, (((0,), (0,)), ((), ())), preferred_e...  10.8 us
  transfers between devices with their start and end apart: 12, of which 12 were waited for; matrix products, arithmetic and copies ran while one was open for 2% of the time, Pallas kernels for 0%

commit v1 on v0

v1 whole, which is shorter than its diff:
```python
import functools

import jax
import jax.numpy as jnp
from jax import lax
from jax.experimental import pallas as pl
from jax.experimental.pallas import tpu as pltpu
from jax.sharding import PartitionSpec as P

norm_eps = 1e-06
MESH = pl.DeviceIdType.MESH
CHUNK = 64
PIECES = 4
bf16, f32 = jnp.bfloat16, jnp.float32
NT = (((1,), (1,)), ((), ()))
TN = (((0,), (0,)), ((), ()))


def kernel(
    sections, shards, chunks,
    acts, gain, wt_shard, head, pool, unpool, counts, labels,
    din, dproj, dgain,
    weight, grads, normed_own, normed_all, inv_rms, back_s, total, gain_acc, gain_all, top_g,
    local_sem, w_send, w_recv, n_send, n_recv, c_send, c_recv, g_send, g_recv, d_send, d_recv,
):
    sec = lax.axis_index("section")
    me = lax.axis_index("fsdp")
    top = sections - 1
    chips = shards // 2
    chip, core = me // 2, lax.rem(me, 2)
    pair = chip * 2 + 1 - core
    width = gain.shape[1]
    blk = width // shards
    rows = CHUNK
    is_top = sec == top

    def ahead(d):
        return lax.rem(chip + d, chips) * 2 + core

    def behind(d, own_core=True):
        return lax.rem(chip + chips - d, chips) * 2 + (core if own_core else 1 - core)

    barrier = pltpu.get_barrier_semaphore()
    for d in range(1, shards):
        pl.semaphore_signal(barrier, 1, device_id=(sec, lax.rem(me + d, shards)), device_id_type=MESH)

    @pl.when(sec > 0)
    def _():
        pl.semaphore_signal(barrier, 1, device_id=(sec - 1, me), device_id_type=MESH)

    @pl.when(sec < top)
    def _():
        pl.semaphore_signal(barrier, 1, device_id=(sec + 1, me), device_id_type=MESH)

    pl.semaphore_wait(
        barrier, shards - 1 + jnp.where(sec > 0, 1, 0) + jnp.where(sec < top, 1, 0)
    )

    def remote(src, dst, send, recv, dev):
        return pltpu.make_async_remote_copy(
            src_ref=src, dst_ref=dst, send_sem=send, recv_sem=recv,
            device_id=dev, device_id_type=MESH,
        )

    piece = width // PIECES

    def w_copy(p, kind, d, src_slot, target, own=False):
        span = pl.ds(p * piece, piece)
        n = 0 if kind == 0 else (d if kind == 1 else chips - 1 + d)
        src = wt_shard.at[span] if own else weight.at[src_slot, span]
        return remote(src, weight.at[src_slot, span], w_send.at[p, n], w_recv.at[p, n], (sec, target))

    own_w = pltpu.make_async_copy(wt_shard, weight.at[me], local_sem)
    own_w.start()
    for p in range(PIECES):
        for d in range(1, chips):
            w_copy(p, 1, d, me, ahead(d), own=True).start()
    for p in range(PIECES):
        w_copy(p, 0, 0, me, pair, own=True).start()

    def prep(k, carry):
        x = acts[k].astype(f32)
        inv = lax.rsqrt(jnp.mean(x * x, -1, keepdims=True) + norm_eps)
        inv_rms[k] = inv
        for b in range(shards):
            cols = slice(b * blk, (b + 1) * blk)
            normed_own[b, k] = (acts[k, :, cols].astype(f32) * inv * gain[:, cols]).astype(bf16)
        normed_all[k, me] = normed_own[me, k]
        return carry

    lax.fori_loop(0, chunks, prep, 0)
    gain_acc[...] = jnp.zeros_like(gain_acc)
    total[...] = jnp.zeros_like(total)

    for p in range(PIECES):
        for d in range(1, chips):
            w_copy(p, 1, d, behind(d), ahead(d)).wait_recv()
            w_copy(p, 2, d, behind(d), pair).start()
    for p in range(PIECES):
        w_copy(p, 0, 0, pair, pair).wait_recv()
        for d in range(1, chips):
            w_copy(p, 2, d, behind(d, False), pair).wait_recv()
    own_w.wait()

    def n_copy(d, src_slot, dst_slot):
        return remote(
            normed_own.at[src_slot], normed_all.at[:, dst_slot],
            n_send.at[d - 1], n_recv.at[d - 1], (sec, lax.rem(me + d, shards)),
        )

    for d in range(1, shards):
        n_copy(d, lax.rem(me + d, shards), me).start()

    @pl.when(is_top)
    def _():
        logits = 0.0
        sum_hi = []
        for b in range(shards):
            cols = slice(b * blk, (b + 1) * blk)
            pn = jnp.zeros((counts.shape[0], blk), f32)
            for k in range(chunks):
                pn = pn + jnp.dot(pool[k], normed_own[b, k], preferred_element_type=f32)
            hi = pn.astype(bf16)
            sum_hi.append(jnp.concatenate([hi, (pn - hi.astype(f32)).astype(bf16)], 0))
        for b in range(shards):
            cols = slice(b * blk, (b + 1) * blk)
            y = jnp.zeros((2 * counts.shape[0], blk), f32)
            for c in range(shards):
                y = y + lax.dot_general(
                    sum_hi[c], weight[c, cols, :], NT, preferred_element_type=f32
                )
            pooled = y[: counts.shape[0]] + y[counts.shape[0] :]
            for k in range(chunks):
                pooled = pooled + jnp.dot(pool[k], acts[k, :, cols], preferred_element_type=f32)
            pooled = (pooled / counts[...]).astype(bf16)
            logits = logits + jnp.dot(pooled, head[cols, :], preferred_element_type=f32)
        classes = lax.broadcasted_iota(jnp.int32, logits.shape, 1)
        target = jnp.where(classes == labels[...], 1.0, 0.0)
        dlogit = (jax.nn.sigmoid(logits) - target).astype(bf16)
        for b in range(shards):
            cols = slice(b * blk, (b + 1) * blk)
            dpool = lax.dot_general(dlogit, head[cols, :], NT, preferred_element_type=f32)
            top_g[:, cols] = (dpool / counts[...]).astype(bf16)

    def c_copy(k):
        return remote(din.at[k], grads.at[k, me], c_send.at[k], c_recv.at[k], (sec - 1, me))

    def g_copy(k, kind, d, slot, target):
        n = 0 if kind == 0 else (d if kind == 1 else chips - 1 + d)
        return remote(
            grads.at[k, slot], grads.at[k, slot], g_send.at[k, n], g_recv.at[k, n], (sec, target)
        )

    def relay(k):
        for d in range(1, chips):
            g_copy(k, 1, d, behind(d), ahead(d)).wait_recv()
            g_copy(k, 2, d, behind(d), pair).start()

    def accumulate(k):
        g_copy(k, 0, 0, pair, pair).wait_recv()
        for d in range(1, chips):
            g_copy(k, 2, d, behind(d, False), pair).wait_recv()
        lhs = normed_all[k].reshape(shards * rows, blk)
        for b in range(4):
            cols = slice(b * (width // 4), (b + 1) * (width // 4))
            rhs = grads[k, :, :, cols].reshape(shards * rows, width // 4)
            total[:, cols] += lax.dot_general(lhs, rhs, TN, preferred_element_type=f32)

    def step(k, carry):
        @pl.when(is_top)
        def _():
            grads[k, me] = jnp.dot(unpool[k], top_g[...], preferred_element_type=f32).astype(bf16)

        @pl.when(sec < top)
        def _():
            c_copy(k).wait_recv()

        g_copy(k, 0, 0, me, pair).start()
        for d in range(1, chips):
            g_copy(k, 1, d, me, ahead(d)).start()

        inv = inv_rms[k]
        dots = jnp.zeros((rows, 1), f32)
        for b in range(shards):
            cols = slice(b * blk, (b + 1) * blk)
            back = jnp.dot(grads[k, me], weight[b], preferred_element_type=f32)
            back_s[:, cols] = back
            prod = back * (acts[k, :, cols].astype(f32) * inv)
            gain_acc[:, cols] += jnp.sum(prod, 0, keepdims=True)
            dots = dots + jnp.sum(prod * gain[:, cols], -1, keepdims=True)
        mean = dots / width
        for b in range(shards):
            cols = slice(b * blk, (b + 1) * blk)
            x_hat = acts[k, :, cols].astype(f32) * inv
            through = inv * (back_s[:, cols] * gain[:, cols] - x_hat * mean)
            din[k, :, cols] = (grads[k, me, :, cols].astype(f32) + through).astype(bf16)

        @pl.when(sec > 0)
        def _():
            c_copy(k).start()

        @pl.when(jnp.logical_and(sec < top, k >= 1))
        def _():
            relay(k - 1)

        @pl.when(jnp.logical_and(sec < top, k == 2))
        def _():
            for d in range(1, shards):
                n_copy(d, me, lax.rem(me + shards - d, shards)).wait_recv()

        @pl.when(jnp.logical_and(sec < top, k >= 2))
        def _():
            accumulate(k - 2)

        return carry

    lax.fori_loop(0, chunks, step, 0)

    def d_copy(d, slot):
        return remote(
            gain_acc, gain_all.at[slot], d_send.at[d - 1], d_recv.at[d - 1],
            (sec, lax.rem(me + d, shards)),
        )

    for d in range(1, shards):
        d_copy(d, me).start()

    def relay_step(k, carry):
        relay(k)
        return carry

    def accumulate_step(k, carry):
        accumulate(k)
        return carry

    @pl.when(is_top)
    def _():
        for d in range(1, shards):
            n_copy(d, me, lax.rem(me + shards - d, shards)).wait_recv()
        lax.fori_loop(0, chunks - 1, relay_step, 0)
        lax.fori_loop(0, chunks - 2, accumulate_step, 0)

    relay(chunks - 1)
    lax.fori_loop(chunks - 2, chunks, accumulate_step, 0)
    dproj[...] = total[...].astype(bf16)

    gain_all[me] = gain_acc[...]
    for d in range(1, shards):
        d_copy(d, lax.rem(me + shards - d, shards)).wait_recv()
    dgain[...] = jnp.sum(gain_all[...], 0)

    for p in range(PIECES):
        w_copy(p, 0, 0, me, pair, own=True).wait_send()
        for d in range(1, chips):
            w_copy(p, 1, d, me, ahead(d), own=True).wait_send()
            w_copy(p, 2, d, behind(d), pair).wait_send()
    for d in range(1, shards):
        n_copy(d, lax.rem(me + d, shards), me).wait_send()
        d_copy(d, me).wait_send()

    def sent(k, carry):
        @pl.when(sec > 0)
        def _():
            c_copy(k).wait_send()

        g_copy(k, 0, 0, me, pair).wait_send()
        for d in range(1, chips):
            g_copy(k, 1, d, me, ahead(d)).wait_send()
            g_copy(k, 2, d, behind(d), pair).wait_send()
        return carry

    lax.fori_loop(0, chunks, sent, 0)


def per_device(sections, shards, acts, gains, proj, head, segs, labels):
    tokens, width = acts.shape[1:]
    batches, rows = segs.shape
    cands = labels.shape[1]
    classes = head.shape[1]
    blk = proj.shape[1]
    chunks = tokens // CHUNK
    chips = shards // 2
    every = batches * cands
    own = segs.reshape(-1) + cands * (jnp.arange(tokens, dtype=jnp.int32) // rows)
    hit = own[:, None] == jnp.arange(every, dtype=jnp.int32)[None, :]
    counts = jnp.sum(hit.astype(f32), 0)[:, None]
    unpool = hit.astype(bf16).reshape(chunks, CHUNK, every)
    pool = unpool.transpose(0, 2, 1)
    vmem = pl.BlockSpec(memory_space=pltpu.VMEM)
    dma = pltpu.SemaphoreType.DMA
    din, dproj, dgain = pl.pallas_call(
        functools.partial(kernel, sections, shards, chunks),
        out_shape=(
            jax.ShapeDtypeStruct((chunks, CHUNK, width), bf16),
            jax.ShapeDtypeStruct((blk, width), bf16),
            jax.ShapeDtypeStruct((1, width), f32),
        ),
        in_specs=[vmem, vmem, pl.BlockSpec(memory_space=pl.ANY)] + [vmem] * 5,
        out_specs=(vmem, vmem, vmem),
        scratch_shapes=[
            pltpu.VMEM((shards, width, blk), bf16),
            pltpu.VMEM((chunks, shards, CHUNK, width), bf16),
            pltpu.VMEM((shards, chunks, CHUNK, blk), bf16),
            pltpu.VMEM((chunks, shards, CHUNK, blk), bf16),
            pltpu.VMEM((chunks, CHUNK, 1), f32),
            pltpu.VMEM((CHUNK, width), f32),
            pltpu.VMEM((blk, width), f32),
            pltpu.VMEM((1, width), f32),
            pltpu.VMEM((shards, 1, width), f32),
            pltpu.VMEM((every, width), bf16),
            dma,
            dma((PIECES, 2 * chips - 1)),
            dma((PIECES, 2 * chips - 1)),
            dma((shards - 1,)),
            dma((shards - 1,)),
            dma((chunks,)),
            dma((chunks,)),
            dma((chunks, 2 * chips - 1)),
            dma((chunks, 2 * chips - 1)),
            dma((shards - 1,)),
            dma((shards - 1,)),
        ],
        compiler_params=pltpu.CompilerParams(
            collective_id=0, has_side_effects=True, vmem_limit_bytes=63 * 1024 * 1024
        ),
        cost_estimate=pl.CostEstimate(
            flops=4 * tokens * width * width, bytes_accessed=16 * width * width, transcendentals=0
        ),
    )(
        acts[0].reshape(chunks, CHUNK, width),
        gains,
        proj[0].T,
        head,
        pool,
        unpool,
        counts,
        labels.reshape(-1, 1),
    )
    return din.reshape(1, tokens, width), dproj[None], dgain


def solution(mesh):
    return jax.shard_map(
        functools.partial(per_device, mesh.shape["section"], mesh.shape["fsdp"]),
        mesh=mesh,
        in_specs=(
            P("section", "fsdp", None),
            P("section", None),
            P("section", "fsdp", None),
            P(),
            P("fsdp", None),
            P("fsdp", None),
        ),
        out_specs=(P("section", "fsdp", None), P("section", "fsdp", None), P("section", None)),
        check_vma=False,
    )
```

time: 489 us -> 203 us (0.42)
  waiting for transfers between devices: 391 us -> 0 us
  Pallas kernels: 0 us -> 187 us
  matrix products: 31.3 us -> 0 us
  other arithmetic: 25.6 us -> 1.63 us
  between operations: 14.1 us -> 0.65 us
  starting transfers between devices: 12.9 us -> 0 us
  local copies, waits for them, and re-layouts: 6.23 us -> 12.9 us
  blocking collectives: 6.67 us -> 0 us
    ppermute x10 -> x0, waiting for transfers between devices: 276 us -> none  [from_behind(): return lax.ppermute(value, axis, pairs)]
    pallas_call x0 -> x1, Pallas kernels: none -> 187 us  [per_device(): pl.pallas_call(functools.partial(kernel, sections, shards, chunks), out_s...]
    reduce_scatter x1 -> x0, waiting for transfers between devices: 61.5 us -> none  [per_device(): lax.psum_scatter(lax.dot_general(normed, flat_grads, (((0,), (0,)), ((),...]
    all_gather x1 -> x0, waiting for transfers between devices: 53 us -> none  [per_device(): weight = lax.all_gather(proj[0], 'fsdp', axis=0, tiled=True)]
    dot_general x4 -> x0, matrix products: 31.3 us -> none  [the longest x3 20.5 us: backward_one(): lax.dot_general(grad_in, weight, (((1,), (1,)), ((), ())), preferred_elem...]
    dynamic_update_slice x6 -> x0, other arithmetic: 16.1 us -> none  [the longest x3 9.04 us: backward_one(): din = lax.dynamic_update_index_in_dim(din, layer_grad, mb_index, 0)]
    ppermute x10 -> x0, starting transfers between devices: 12.8 us -> none  [from_behind(): return lax.ppermute(value, axis, pairs)]
    unnamed x8, local copies, waits for them, and re-layouts: 0.02 us -> 9.35 us
  transfers between devices with their start and end apart: 12 -> 0, of which waited for: 12 -> 0; matrix products, arithmetic and copies ran while one was open for 2% -> 0% of each run, Pallas kernels for 0% -> 0%
where the time goes in v1:
time: 203 us; the launch traced here: 202 us
  Pallas kernels  187 us (92%)
  local copies, waits for them, and re-layouts  12.9 us (6%)
    pallas_call x1, Pallas kernels, per_device(): pl.pallas_call(functools.partial(kernel, sections, shards, chunks), out_s...  187 us
    unnamed x8, local copies, waits for them, and re-layouts  9.35 us

profile of v1, /device:TPU:0, one launch (start us, length us, event | category | flops | bytes accessed | tf_op | source)
XLA Modules:
  0.0 202.3 jit_solution(18088505151991131603)
XLA Ops:
  0.6 0.8 reshape.50
  1.4 0.1 convert_reduce_fusion
  1.5 0.8 reshape.49
  2.3 0.7 copy.13.counts
  3.0 1.4 reshape.53.labels
  4.4 0.7 fusion.1.pool
  5.1 0.8 fusion.unpool
  5.9 3.9 %copy.12 = bf16[1,512,2048]{1,2,0:T(8,128)(2,1)} copy(bf16[1,512,2048]{2,1,0:T(8,128)(2,1)} %param.8) | data formatting | bytes 4194304 | tf_op args[2]
  9.8 187.1 %shard_map.85 = (bf16[9,64,2048]{2,1,0:T(8,128)(2,1)}, bf16[512,2048]{1,0:T(8,128)(2,1)}, f32[1,2048]{1,0:T(1,128)}) custom-call(bf16[9,64,2048]{2,1,0:T(8,128)(2,1)} %bitcast.11, f32[1,2048]{1,0:T(1,128)} %gain.1, bf16[2048,512]{1,0:T(8,128)(2,1)} %bitcast.9, bf16[2048,512]{1,0:T(8,128)(2,1)} %head.1, bf16[9,48,64]{2,1,0:T(8,128)(2,1)} %fusion.1.pool, ...), custom_call_target="tpu_custom_call" | custom-call | flops 9663676416 | bytes 67108864 | tf_op jit(solution)/shard_map/pallas_call | solution.py:291
  196.9 0.0 copy-start
  196.9 3.5 %copy.18 = bf16[1,576,2048]{2,1,0:T(8,128)(2,1)} copy(bf16[1,576,2048]{2,1,0:T(8,128)(2,1)} %bitcast.7) | data formatting | bytes 4718592
  200.4 0.0 copy-done
  200.4 0.0 copy-start.1
  200.4 1.3 copy.19
  201.7 0.0 copy-done.1
  201.7 0.6 copy.20
  (2 shorter events, 0.0 us)
Async XLA Ops:
  196.9 3.5 %copy-start = (bf16[512,2048]{1,0:T(8,128)(2,1)S(1)}, bf16[512,2048]{1,0:T(8,128)(2,1)}, u32[]{:S(2)}) copy-start(bf16[512,2048]{1,0:T(8,128)(2,1)} %get-tuple-element.7) | copy-start | bytes 6291460
  200.4 1.3 copy-start.1

commit v2 on v1

v2 whole, which is shorter than its diff:
```python
import functools

import jax
import jax.numpy as jnp
from jax import lax
from jax.experimental import pallas as pl
from jax.experimental.pallas import tpu as pltpu
from jax.sharding import PartitionSpec as P

norm_eps = 1e-06
MESH = pl.DeviceIdType.MESH
CHUNK = 64
PIECES = 4
bf16, f32 = jnp.bfloat16, jnp.float32
NT = (((1,), (1,)), ((), ()))
TN = (((0,), (0,)), ((), ()))


def kernel(
    sections, shards, chunks,
    acts_hbm, gain, wt_shard, head_hbm, segs, labels,
    din, dproj, dgain,
    acts, head, weight, grads, normed_own, normed_all, inv_rms, back_s, total, gain_acc, gain_all,
    pool, part_out, part_in,
    local_sem, w_send, w_recv, n_send, n_recv, c_send, c_recv, g_send, g_recv, d_send, d_recv,
    t_send, t_recv,
):
    sec = lax.axis_index("section")
    me = lax.axis_index("fsdp")
    top = sections - 1
    chips = shards // 2
    chip, core = me // 2, lax.rem(me, 2)
    pair = chip * 2 + 1 - core
    width = gain.shape[1]
    blk = width // shards
    rows = CHUNK
    is_top = sec == top

    def ahead(d):
        return lax.rem(chip + d, chips) * 2 + core

    def behind(d, own_core=True):
        return lax.rem(chip + chips - d, chips) * 2 + (core if own_core else 1 - core)

    own_acts = pltpu.make_async_copy(acts_hbm, acts, local_sem.at[1])
    own_acts.start()
    own_w = pltpu.make_async_copy(wt_shard, weight.at[me], local_sem.at[0])
    own_w.start()
    own_head = pltpu.make_async_copy(head_hbm, head, local_sem.at[2])

    @pl.when(is_top)
    def _():
        own_head.start()

    barrier = pltpu.get_barrier_semaphore()
    for d in range(1, shards):
        pl.semaphore_signal(barrier, 1, device_id=(sec, lax.rem(me + d, shards)), device_id_type=MESH)

    @pl.when(sec > 0)
    def _():
        pl.semaphore_signal(barrier, 1, device_id=(sec - 1, me), device_id_type=MESH)

    @pl.when(sec < top)
    def _():
        pl.semaphore_signal(barrier, 1, device_id=(sec + 1, me), device_id_type=MESH)

    pl.semaphore_wait(
        barrier, shards - 1 + jnp.where(sec > 0, 1, 0) + jnp.where(sec < top, 1, 0)
    )

    def remote(src, dst, send, recv, dev):
        return pltpu.make_async_remote_copy(
            src_ref=src, dst_ref=dst, send_sem=send, recv_sem=recv,
            device_id=dev, device_id_type=MESH,
        )

    piece = width // PIECES

    def w_copy(p, kind, d, src_slot, target, own=False):
        span = pl.ds(p * piece, piece)
        n = 0 if kind == 0 else (d if kind == 1 else chips - 1 + d)
        src = wt_shard.at[span] if own else weight.at[src_slot, span]
        return remote(src, weight.at[src_slot, span], w_send.at[p, n], w_recv.at[p, n], (sec, target))

    @pl.when(sec < top)
    def _():
        for p in range(PIECES):
            for d in range(1, chips):
                w_copy(p, 1, d, me, ahead(d), own=True).start()
        for p in range(PIECES):
            w_copy(p, 0, 0, me, pair, own=True).start()

    own_acts.wait()

    def prep(k, carry):
        x = acts[k].astype(f32)
        inv = lax.rsqrt(jnp.mean(x * x, -1, keepdims=True) + norm_eps)
        inv_rms[k] = inv
        for b in range(shards):
            cols = slice(b * blk, (b + 1) * blk)
            normed_own[b, k] = (acts[k, :, cols].astype(f32) * inv * gain[:, cols]).astype(bf16)
        @pl.when(sec < top)
        def _():
            normed_all[k, me] = normed_own[me, k]

        return carry

    lax.fori_loop(0, chunks, prep, 0)
    gain_acc[...] = jnp.zeros_like(gain_acc)
    total[...] = jnp.zeros_like(total)

    own_w.wait()

    def n_copy(d, src_slot, dst_slot):
        return remote(
            normed_own.at[src_slot], normed_all.at[:, dst_slot],
            n_send.at[d - 1], n_recv.at[d - 1], (sec, lax.rem(me + d, shards)),
        )

    @pl.when(sec < top)
    def _():
        for p in range(PIECES):
            for d in range(1, chips):
                w_copy(p, 1, d, behind(d), ahead(d)).wait_recv()
                w_copy(p, 2, d, behind(d), pair).start()
        for p in range(PIECES):
            w_copy(p, 0, 0, pair, pair).wait_recv()
            for d in range(1, chips):
                w_copy(p, 2, d, behind(d, False), pair).wait_recv()
        for d in range(1, shards):
            n_copy(d, lax.rem(me + d, shards), me).start()

    batches, cands = labels.shape
    every = batches * cands
    per_batch = segs.shape[1] // rows
    classes = head.shape[1]
    quarter = width // 4

    def t_copy(n, src, dst, d):
        return remote(
            src, dst, t_send.at[n, d - 1], t_recv.at[n, d - 1], (sec, lax.rem(me + d, shards))
        )

    def sums_out(d):
        return t_copy(0, normed_all.at[0:2, lax.rem(me + d, shards), 0:every],
                      normed_all.at[2:4, me, 0:every], d)

    def parts_out(d):
        return t_copy(1, part_out.at[lax.rem(me + d, shards), :, 0:classes],
                      part_in.at[me, :, 0:classes], d)

    def grad_out(d):
        mine = grads.at[0, me, 0:every]
        return t_copy(2, mine, mine, d)

    def backs_out(d):
        return t_copy(3, part_out.at[lax.rem(me + d, shards), :, 0:blk],
                      part_in.at[me, :, 0:blk], d)

    def split(value):
        hi = value.astype(bf16)
        return hi, (value - hi.astype(f32)).astype(bf16)

    def flat(ref_value):
        return ref_value.reshape(shards * every, ref_value.shape[-1])

    @pl.when(is_top)
    def _():
        slots = lax.broadcasted_iota(jnp.int32, (every, rows), 0)
        counts = jnp.zeros((every, 1), f32)
        for k in range(chunks):
            m, at = k // per_batch, (k % per_batch) * rows
            hit = jnp.where(segs[m : m + 1, at : at + rows] + cands * m == slots, 1.0, 0.0)
            counts = counts + jnp.sum(hit, -1, keepdims=True)
            pool[k] = hit.astype(bf16)
        for b in range(shards):
            sums = jnp.zeros((every, blk), f32)
            for k in range(chunks):
                sums = sums + jnp.dot(pool[k], normed_own[b, k], preferred_element_type=f32)
            hi, lo = split(sums)
            normed_all[0, b, 0:every] = hi
            normed_all[1, b, 0:every] = lo
        for d in range(1, shards):
            sums_out(d).start()
        normed_all[2, me, 0:every] = normed_all[0, me, 0:every]
        normed_all[3, me, 0:every] = normed_all[1, me, 0:every]
        own_head.wait()
        logits = jnp.zeros((2 * every, classes), f32)
        for b in range(4):
            cols = slice(b * quarter, (b + 1) * quarter)
            sums = jnp.zeros((every, quarter), f32)
            for k in range(chunks):
                sums = sums + jnp.dot(pool[k], acts[k, :, cols], preferred_element_type=f32)
            logits = logits + jnp.dot(
                jnp.concatenate(split(sums), 0), head[cols, :], preferred_element_type=f32
            )
        logits = logits[:every] + logits[every:]
        for d in range(1, shards):
            sums_out(d).wait_recv()
        both = jnp.concatenate([flat(normed_all[n, :, 0:every]) for n in (2, 3)], 0)
        part = jnp.zeros((shards * every, classes), f32)
        for b in range(4):
            cols = slice(b * quarter, (b + 1) * quarter)
            y = lax.dot_general(both, weight[me, cols, :], NT, preferred_element_type=f32)
            y = (y[: shards * every] + y[shards * every :]).astype(bf16)
            part = part + jnp.dot(y, head[cols, :], preferred_element_type=f32)
        part_out[:, :, 0:classes] = part.reshape(shards, every, classes)
        for d in range(1, shards):
            parts_out(d).start()
        part_in[me] = part_out[me]
        for d in range(1, shards):
            parts_out(d).wait_recv()
        logits = (logits + jnp.sum(part_in[:, :, 0:classes], 0)) / counts
        lanes = lax.broadcasted_iota(jnp.int32, (cands, cands), 1)
        diagonal = lanes == lax.broadcasted_iota(jnp.int32, (cands, cands), 0)
        target = []
        for m in range(batches):
            own = jnp.where(diagonal, labels[m : m + 1, :].astype(f32), 0.0)
            target.append(jnp.sum(own, -1, keepdims=True))
        target = jnp.concatenate(target, 0).astype(jnp.int32)
        target = lax.broadcasted_iota(jnp.int32, (every, classes), 1) == target
        dlogit = (jax.nn.sigmoid(logits) - jnp.where(target, 1.0, 0.0)).astype(bf16)
        for b in range(4):
            cols = slice(b * quarter, (b + 1) * quarter)
            dpool = lax.dot_general(dlogit, head[cols, :], NT, preferred_element_type=f32)
            grads[0, me, 0:every, cols] = (dpool / counts).astype(bf16)
        for d in range(1, shards):
            grad_out(d).start()
        for d in range(1, shards):
            grad_out(d).wait_recv()
        for d in range(1, shards):
            parts_out(d).wait_send()
        part_out[:, :, 0:blk] = jnp.dot(
            flat(grads[0, :, 0:every]), weight[me], preferred_element_type=f32
        ).reshape(shards, every, blk)
        for d in range(1, shards):
            backs_out(d).start()
        part_in[me] = part_out[me]
        for d in range(1, shards):
            backs_out(d).wait_recv()
        for b in range(shards):
            hi, lo = split(part_in[b, :, 0:blk])
            normed_all[4, b, 0:every] = hi
            normed_all[5, b, 0:every] = lo

    def c_copy(k):
        return remote(din.at[k], grads.at[k, me], c_send.at[k], c_recv.at[k], (sec - 1, me))

    def g_copy(k, kind, d, slot, target):
        n = 0 if kind == 0 else (d if kind == 1 else chips - 1 + d)
        return remote(
            grads.at[k, slot], grads.at[k, slot], g_send.at[k, n], g_recv.at[k, n], (sec, target)
        )

    def relay(k):
        for d in range(1, chips):
            g_copy(k, 1, d, behind(d), ahead(d)).wait_recv()
            g_copy(k, 2, d, behind(d), pair).start()

    def accumulate(k):
        g_copy(k, 0, 0, pair, pair).wait_recv()
        for d in range(1, chips):
            g_copy(k, 2, d, behind(d, False), pair).wait_recv()
        lhs = normed_all[k].reshape(shards * rows, blk)
        for b in range(4):
            cols = slice(b * (width // 4), (b + 1) * (width // 4))
            rhs = grads[k, :, :, cols].reshape(shards * rows, width // 4)
            total[:, cols] += lax.dot_general(lhs, rhs, TN, preferred_element_type=f32)

    def section_back(k, back_of, grad_of):
        inv = inv_rms[k]
        dots = jnp.zeros((rows, 1), f32)
        for b in range(shards):
            cols = slice(b * blk, (b + 1) * blk)
            back = back_of(b)
            back_s[:, cols] = back
            prod = back * (acts[k, :, cols].astype(f32) * inv)
            gain_acc[:, cols] += jnp.sum(prod, 0, keepdims=True)
            dots = dots + jnp.sum(prod * gain[:, cols], -1, keepdims=True)
        mean = dots / width
        for b in range(shards):
            cols = slice(b * blk, (b + 1) * blk)
            x_hat = acts[k, :, cols].astype(f32) * inv
            through = inv * (back_s[:, cols] * gain[:, cols] - x_hat * mean)
            din[k, :, cols] = (grad_of(cols) + through).astype(bf16)

        @pl.when(sec > 0)
        def _():
            c_copy(k).start()

    def top_step(k, carry):
        def pick(value):
            return lax.dot_general(pool[k], value, TN, preferred_element_type=f32)

        section_back(
            k,
            lambda b: pick(normed_all[4, b, 0:every]) + pick(normed_all[5, b, 0:every]),
            lambda cols: pick(grads[0, me, 0:every, cols]),
        )
        return carry

    def step(k, carry):
        c_copy(k).wait_recv()
        g_copy(k, 0, 0, me, pair).start()
        for d in range(1, chips):
            g_copy(k, 1, d, me, ahead(d)).start()
        section_back(
            k,
            lambda b: jnp.dot(grads[k, me], weight[b], preferred_element_type=f32),
            lambda cols: grads[k, me, :, cols].astype(f32),
        )

        @pl.when(k >= 1)
        def _():
            relay(k - 1)

        @pl.when(k == 2)
        def _():
            for d in range(1, shards):
                n_copy(d, me, lax.rem(me + shards - d, shards)).wait_recv()

        @pl.when(k >= 2)
        def _():
            accumulate(k - 2)

        return carry

    @pl.when(is_top)
    def _():
        lax.fori_loop(0, chunks, top_step, 0)

    @pl.when(sec < top)
    def _():
        lax.fori_loop(0, chunks, step, 0)

    def d_copy(d, slot):
        return remote(
            gain_acc, gain_all.at[slot], d_send.at[d - 1], d_recv.at[d - 1],
            (sec, lax.rem(me + d, shards)),
        )

    for d in range(1, shards):
        d_copy(d, me).start()

    @pl.when(is_top)
    def _():
        every_grad = flat(grads[0, :, 0:every])
        for n in (2, 3):
            sums = flat(normed_all[n, :, 0:every])
            for b in range(4):
                cols = slice(b * quarter, (b + 1) * quarter)
                total[:, cols] += lax.dot_general(
                    sums, every_grad[:, cols], TN, preferred_element_type=f32
                )

    def accumulate_step(k, carry):
        accumulate(k)
        return carry

    @pl.when(sec < top)
    def _():
        relay(chunks - 1)
        lax.fori_loop(chunks - 2, chunks, accumulate_step, 0)

    dproj[...] = total[...].astype(bf16)

    gain_all[me] = gain_acc[...]
    for d in range(1, shards):
        d_copy(d, lax.rem(me + shards - d, shards)).wait_recv()
    dgain[...] = jnp.sum(gain_all[...], 0)

    for d in range(1, shards):
        d_copy(d, me).wait_send()

    @pl.when(is_top)
    def _():
        for d in range(1, shards):
            sums_out(d).wait_send()
            grad_out(d).wait_send()
            backs_out(d).wait_send()

    @pl.when(sec < top)
    def _():
        for p in range(PIECES):
            w_copy(p, 0, 0, me, pair, own=True).wait_send()
            for d in range(1, chips):
                w_copy(p, 1, d, me, ahead(d), own=True).wait_send()
                w_copy(p, 2, d, behind(d), pair).wait_send()
        for d in range(1, shards):
            n_copy(d, lax.rem(me + d, shards), me).wait_send()

    def sent(k, carry):
        @pl.when(sec > 0)
        def _():
            c_copy(k).wait_send()

        @pl.when(sec < top)
        def _():
            g_copy(k, 0, 0, me, pair).wait_send()
            for d in range(1, chips):
                g_copy(k, 1, d, me, ahead(d)).wait_send()
                g_copy(k, 2, d, behind(d), pair).wait_send()

        return carry

    lax.fori_loop(0, chunks, sent, 0)


def per_device(sections, shards, acts, gains, proj, head, segs, labels):
    tokens, width = acts.shape[1:]
    batches, rows = segs.shape
    cands = labels.shape[1]
    classes = head.shape[1]
    blk = proj.shape[1]
    chunks = tokens // CHUNK
    chips = shards // 2
    every = batches * cands
    vmem = pl.BlockSpec(memory_space=pltpu.VMEM)
    hbm = pl.BlockSpec(memory_space=pl.ANY)
    dma = pltpu.SemaphoreType.DMA
    din, dproj, dgain = pl.pallas_call(
        functools.partial(kernel, sections, shards, chunks),
        out_shape=(
            jax.ShapeDtypeStruct((chunks, CHUNK, width), bf16),
            jax.ShapeDtypeStruct((blk, width), bf16),
            jax.ShapeDtypeStruct((1, width), f32),
        ),
        in_specs=[hbm, vmem, hbm, hbm, vmem, vmem],
        out_specs=(vmem, vmem, vmem),
        scratch_shapes=[
            pltpu.VMEM((chunks, CHUNK, width), bf16),
            pltpu.VMEM((width, classes), bf16),
            pltpu.VMEM((shards, width, blk), bf16),
            pltpu.VMEM((chunks, shards, CHUNK, width), bf16),
            pltpu.VMEM((shards, chunks, CHUNK, blk), bf16),
            pltpu.VMEM((chunks, shards, CHUNK, blk), bf16),
            pltpu.VMEM((chunks, CHUNK, 1), f32),
            pltpu.VMEM((CHUNK, width), f32),
            pltpu.VMEM((blk, width), f32),
            pltpu.VMEM((1, width), f32),
            pltpu.VMEM((shards, 1, width), f32),
            pltpu.VMEM((chunks, every, CHUNK), bf16),
            pltpu.VMEM((shards, every, max(classes, blk)), f32),
            pltpu.VMEM((shards, every, max(classes, blk)), f32),
            dma((3,)),
            dma((PIECES, 2 * chips - 1)),
            dma((PIECES, 2 * chips - 1)),
            dma((shards - 1,)),
            dma((shards - 1,)),
            dma((chunks,)),
            dma((chunks,)),
            dma((chunks, 2 * chips - 1)),
            dma((chunks, 2 * chips - 1)),
            dma((shards - 1,)),
            dma((shards - 1,)),
            dma((4, shards - 1)),
            dma((4, shards - 1)),
        ],
        compiler_params=pltpu.CompilerParams(
            collective_id=0, has_side_effects=True, vmem_limit_bytes=127 * 512 * 1024
        ),
        cost_estimate=pl.CostEstimate(
            flops=4 * tokens * width * width, bytes_accessed=16 * width * width, transcendentals=0
        ),
    )(
        acts[0].reshape(chunks, CHUNK, width),
        gains,
        proj[0].T,
        head,
        segs,
        labels,
    )
    return din.reshape(1, tokens, width), dproj[None], dgain


def solution(mesh):
    return jax.shard_map(
        functools.partial(per_device, mesh.shape["section"], mesh.shape["fsdp"]),
        mesh=mesh,
        in_specs=(
            P("section", "fsdp", None),
            P("section", None),
            P("section", "fsdp", None),
            P(),
            P("fsdp", None),
            P("fsdp", None),
        ),
        out_specs=(P("section", "fsdp", None), P("section", "fsdp", None), P("section", None)),
        check_vma=False,
    )
```

time: 203 us -> 196 us (0.966)
  local copies, waits for them, and re-layouts: 12.9 us -> 9.36 us
    reshape x3 -> x0, local copies, waits for them, and re-layouts: 2.9 us -> none  [the longest x2 1.53 us: per_device(): segs.reshape(-1) + cands * (jnp.arange(tokens, dtype=jnp.int32) // rows)]
where the time goes in v2:
time: 196 us; the launch traced here: 195 us
  Pallas kernels  185 us (94%)
  local copies, waits for them, and re-layouts  9.36 us (5%)
    pallas_call x1, Pallas kernels, per_device(): pl.pallas_call(functools.partial(kernel, sections, shards, chunks), out_s...  185 us
    unnamed x8, local copies, waits for them, and re-layouts  9.36 us

profile of v2, /device:TPU:0, one launch (start us, length us, event | category | flops | bytes accessed | tf_op | source)
XLA Modules:
  0.0 195.2 jit_solution(10632387286722987862)
XLA Ops:
  0.6 3.9 %copy.9 = bf16[1,512,2048]{1,2,0:T(8,128)(2,1)} copy(bf16[1,512,2048]{2,1,0:T(8,128)(2,1)} %param.8) | data formatting | bytes 4194304 | tf_op args[2]
  4.6 185.2 %shard_map.85 = (bf16[9,64,2048]{2,1,0:T(8,128)(2,1)}, bf16[512,2048]{1,0:T(8,128)(2,1)}, f32[1,2048]{1,0:T(1,128)}) custom-call(bf16[9,64,2048]{2,1,0:T(8,128)(2,1)} %bitcast.9, f32[1,2048]{1,0:T(1,128)} %gain.1, bf16[2048,512]{1,0:T(8,128)(2,1)} %bitcast.8, bf16[2048,512]{1,0:T(8,128)(2,1)} %head_hbm.1, s32[3,192]{1,0:T(4,128)} %segs.1, s32[3,16]{1,0:T(4,128)} %labels.1), custom_call_target="tpu_custom_call" | custom-call | flops 9663676416 | bytes 67108864 | tf_op jit(solution)/shard_map/pallas_call | solution.py:421
  189.7 0.0 copy-start
  189.7 3.5 %copy.13 = bf16[1,576,2048]{2,1,0:T(8,128)(2,1)} copy(bf16[1,576,2048]{2,1,0:T(8,128)(2,1)} %bitcast.6) | data formatting | bytes 4718592
  193.2 0.0 copy-done
  193.2 0.0 copy-start.1
  193.3 1.3 copy.14
  194.6 0.0 copy-done.1
  194.6 0.6 copy.15
Async XLA Ops:
  189.7 3.5 %copy-start = (bf16[512,2048]{1,0:T(8,128)(2,1)S(1)}, bf16[512,2048]{1,0:T(8,128)(2,1)}, u32[]{:S(2)}) copy-start(bf16[512,2048]{1,0:T(8,128)(2,1)} %get-tuple-element.7) | copy-start | bytes 6291460
  193.2 1.3 copy-start.1

commit v3 on v2

--- a/solution.py
+++ b/solution.py
@@ -10,7 +10,8 @@
 norm_eps = 1e-06
 MESH = pl.DeviceIdType.MESH
 CHUNK = 64
-PIECES = 4
+PIECES = 16
+LENT = 7
 bf16, f32 = jnp.bfloat16, jnp.float32
 NT = (((1,), (1,)), ((), ()))
 TN = (((0,), (0,)), ((), ()))
@@ -21,9 +22,9 @@
     acts_hbm, gain, wt_shard, head_hbm, segs, labels,
     din, dproj, dgain,
     acts, head, weight, grads, normed_own, normed_all, inv_rms, back_s, total, gain_acc, gain_all,
-    pool, part_out, part_in,
+    pool, part_out, part_in, via_in, via_out,
     local_sem, w_send, w_recv, n_send, n_recv, c_send, c_recv, g_send, g_recv, d_send, d_recv,
-    t_send, t_recv,
+    t_send, t_recv, v_send, v_recv,
 ):
     sec = lax.axis_index("section")
     me = lax.axis_index("fsdp")
@@ -35,6 +36,14 @@
     blk = width // shards
     rows = CHUNK
     is_top = sec == top
+    lending = chips == 2 and sections >= 8
+    other = top - 1 - sec
+    borrows = jnp.logical_and(lending, jnp.logical_and(sec >= top - 2, sec < top))
+    lends = jnp.logical_and(lending, sec <= 1)
+    lone = jnp.logical_not(borrows)
+    direct = list(range(PIECES - LENT))
+    lent = list(range(PIECES - LENT, PIECES))
+    order = [p for i in direct for p in (direct[i : i + 1] + lent[i : i + 1])]
 
     def ahead(d):
         return lax.rem(chip + d, chips) * 2 + core
@@ -64,8 +73,16 @@
     def _():
         pl.semaphore_signal(barrier, 1, device_id=(sec + 1, me), device_id_type=MESH)
 
+    @pl.when(jnp.logical_or(borrows, lends))
+    def _():
+        pl.semaphore_signal(barrier, 1, device_id=(other, me), device_id_type=MESH)
+
     pl.semaphore_wait(
-        barrier, shards - 1 + jnp.where(sec > 0, 1, 0) + jnp.where(sec < top, 1, 0)
+        barrier,
+        shards - 1
+        + jnp.where(sec > 0, 1, 0)
+        + jnp.where(sec < top, 1, 0)
+        + jnp.where(jnp.logical_or(borrows, lends), 1, 0),
     )
 
     def remote(src, dst, send, recv, dev):
@@ -82,12 +99,46 @@
         src = wt_shard.at[span] if own else weight.at[src_slot, span]
         return remote(src, weight.at[src_slot, span], w_send.at[p, n], w_recv.at[p, n], (sec, target))
 
+    def v_copy(hop, i):
+        span = pl.ds((PIECES - LENT + i) * piece, piece)
+        if hop == 0:
+            src, dst, dev = wt_shard.at[span], via_in.at[i], (other, me)
+        elif hop == 1:
+            src, dst, dev = via_in.at[i], via_out.at[i], (sec, ahead(1))
+        else:
+            src, dst, dev = via_out.at[i], weight.at[ahead(1), span], (other, me)
+        recv = w_recv.at[PIECES - LENT + i, 1] if hop == 2 else v_recv.at[hop, i]
+        return remote(src, dst, v_send.at[hop, i], recv, dev)
+
+    if lending:
+        @pl.when(borrows)
+        def _():
+            for i in range(LENT):
+                v_copy(0, i).start()
+
+        @pl.when(lends)
+        def _():
+            for i in range(LENT + 1):
+                if i < LENT:
+                    v_copy(0, i).wait_recv()
+                    v_copy(1, i).start()
+                if i > 0:
+                    v_copy(1, i - 1).wait_recv()
+                    v_copy(2, i - 1).start()
+
     @pl.when(sec < top)
     def _():
-        for p in range(PIECES):
+        for p in direct:
             for d in range(1, chips):
                 w_copy(p, 1, d, me, ahead(d), own=True).start()
-        for p in range(PIECES):
+
+        @pl.when(lone)
+        def _():
+            for p in lent:
+                for d in range(1, chips):
+                    w_copy(p, 1, d, me, ahead(d), own=True).start()
+
+        for p in order:
             w_copy(p, 0, 0, me, pair, own=True).start()
 
     own_acts.wait()
@@ -119,7 +170,7 @@
 
     @pl.when(sec < top)
     def _():
-        for p in range(PIECES):
+        for p in order:
             for d in range(1, chips):
                 w_copy(p, 1, d, behind(d), ahead(d)).wait_recv()
                 w_copy(p, 2, d, behind(d), pair).start()
@@ -266,6 +317,12 @@
             cols = slice(b * (width // 4), (b + 1) * (width // 4))
             rhs = grads[k, :, :, cols].reshape(shards * rows, width // 4)
             total[:, cols] += lax.dot_general(lhs, rhs, TN, preferred_element_type=f32)
+
+    lag = jnp.clip(1 + 2 * (sec - (top - 4)), 1, chunks)
+
+    def columns_here():
+        for d in range(1, shards):
+            n_copy(d, me, lax.rem(me + shards - d, shards)).wait_recv()
 
     def section_back(k, back_of, grad_of):
         inv = inv_rms[k]
@@ -310,18 +367,17 @@
             lambda cols: grads[k, me, :, cols].astype(f32),
         )
 
-        @pl.when(k >= 1)
-        def _():
-            relay(k - 1)
-
-        @pl.when(k == 2)
-        def _():
-            for d in range(1, shards):
-                n_copy(d, me, lax.rem(me + shards - d, shards)).wait_recv()
-
-        @pl.when(k >= 2)
-        def _():
-            accumulate(k - 2)
+        @pl.when(k >= lag)
+        def _():
+            relay(k - lag)
+
+        @pl.when(k == lag + 1)
+        def _():
+            columns_here()
+
+        @pl.when(k >= lag + 1)
+        def _():
+            accumulate(k - lag - 1)
 
         return carry
 
@@ -353,14 +409,22 @@
                     sums, every_grad[:, cols], TN, preferred_element_type=f32
                 )
 
+    def relay_step(k, carry):
+        relay(k)
+        return carry
+
     def accumulate_step(k, carry):
         accumulate(k)
         return carry
 
     @pl.when(sec < top)
     def _():
-        relay(chunks - 1)
-        lax.fori_loop(chunks - 2, chunks, accumulate_step, 0)
+        @pl.when(lag + 1 >= chunks)
+        def _():
+            columns_here()
+
+        lax.fori_loop(chunks - lag, chunks, relay_step, 0)
+        lax.fori_loop(jnp.maximum(chunks - lag - 1, 0), chunks, accumulate_step, 0)
 
     dproj[...] = total[...].astype(bf16)
 
@@ -384,10 +448,31 @@
         for p in range(PIECES):
             w_copy(p, 0, 0, me, pair, own=True).wait_send()
             for d in range(1, chips):
+                w_copy(p, 2, d, behind(d), pair).wait_send()
+        for p in direct:
+            for d in range(1, chips):
                 w_copy(p, 1, d, me, ahead(d), own=True).wait_send()
-                w_copy(p, 2, d, behind(d), pair).wait_send()
+
+        @pl.when(lone)
+        def _():
+            for p in lent:
+                for d in range(1, chips):
+                    w_copy(p, 1, d, me, ahead(d), own=True).wait_send()
+
         for d in range(1, shards):
             n_copy(d, lax.rem(me + d, shards), me).wait_send()
+
+    if lending:
+        @pl.when(borrows)
+        def _():
+            for i in range(LENT):
+                v_copy(0, i).wait_send()
+
+        @pl.when(lends)
+        def _():
+            for i in range(LENT):
+                v_copy(1, i).wait_send()
+                v_copy(2, i).wait_send()
 
     def sent(k, carry):
         @pl.when(sec > 0)
@@ -442,6 +527,8 @@
             pltpu.VMEM((chunks, every, CHUNK), bf16),
             pltpu.VMEM((shards, every, max(classes, blk)), f32),
             pltpu.VMEM((shards, every, max(classes, blk)), f32),
+            pltpu.VMEM((LENT, width // PIECES if chips == 2 else 16, blk), bf16),
+            pltpu.VMEM((LENT, width // PIECES if chips == 2 else 16, blk), bf16),
             dma((3,)),
             dma((PIECES, 2 * chips - 1)),
             dma((PIECES, 2 * chips - 1)),
@@ -455,6 +542,8 @@
             dma((shards - 1,)),
             dma((4, shards - 1)),
             dma((4, shards - 1)),
+            dma((3, LENT)),
+            dma((3, LENT)),
         ],
         compiler_params=pltpu.CompilerParams(
             collective_id=0, has_side_effects=True, vmem_limit_bytes=127 * 512 * 1024

time: 196 us -> 178 us (0.908)
  Pallas kernels: 185 us -> 168 us
    pallas_call x1, Pallas kernels: 185 us -> 168 us  [per_device(): pl.pallas_call(functools.partial(kernel, sections, shards, chunks), out_s...]
where the time goes in v3:
time: 178 us
  Pallas kernels  168 us (94%)
  local copies, waits for them, and re-layouts  9.36 us (5%)
    pallas_call x1, Pallas kernels, per_device(): pl.pallas_call(functools.partial(kernel, sections, shards, chunks), out_s...  168 us
    unnamed x8, local copies, waits for them, and re-layouts  9.36 us

profile of v3, /device:TPU:0, one launch (start us, length us, event | category | flops | bytes accessed | tf_op | source)
XLA Modules:
  0.0 177.9 jit_solution(10143162543313773295)
XLA Ops:
  0.6 3.9 %copy.9 = bf16[1,512,2048]{1,2,0:T(8,128)(2,1)} copy(bf16[1,512,2048]{2,1,0:T(8,128)(2,1)} %param.8) | data formatting | bytes 4194304 | tf_op args[2]
  4.6 167.9 %shard_map.85 = (bf16[9,64,2048]{2,1,0:T(8,128)(2,1)}, bf16[512,2048]{1,0:T(8,128)(2,1)}, f32[1,2048]{1,0:T(1,128)}) custom-call(bf16[9,64,2048]{2,1,0:T(8,128)(2,1)} %bitcast.9, f32[1,2048]{1,0:T(1,128)} %gain.1, bf16[2048,512]{1,0:T(8,128)(2,1)} %bitcast.8, bf16[2048,512]{1,0:T(8,128)(2,1)} %head_hbm.1, s32[3,192]{1,0:T(4,128)} %segs.1, s32[3,16]{1,0:T(4,128)} %labels.1), custom_call_target="tpu_custom_call" | custom-call | flops 9663676416 | bytes 67108864 | tf_op jit(solution)/shard_map/pallas_call | solution.py:506
  172.4 0.0 copy-start
  172.4 3.5 %copy.13 = bf16[1,576,2048]{2,1,0:T(8,128)(2,1)} copy(bf16[1,576,2048]{2,1,0:T(8,128)(2,1)} %bitcast.6) | data formatting | bytes 4718592
  175.9 0.0 copy-done
  175.9 0.0 copy-start.1
  175.9 1.3 copy.14
  177.3 0.0 copy-done.1
  177.3 0.6 copy.15
Async XLA Ops:
  172.4 3.5 %copy-start = (bf16[512,2048]{1,0:T(8,128)(2,1)S(1)}, bf16[512,2048]{1,0:T(8,128)(2,1)}, u32[]{:S(2)}) copy-start(bf16[512,2048]{1,0:T(8,128)(2,1)} %get-tuple-element.7) | copy-start | bytes 6291460
  175.9 1.3 copy-start.1

commit v4 on v3

--- a/solution.py
+++ b/solution.py
@@ -11,7 +11,7 @@
 MESH = pl.DeviceIdType.MESH
 CHUNK = 64
 PIECES = 16
-LENT = 7
+LENT = 5
 bf16, f32 = jnp.bfloat16, jnp.float32
 NT = (((1,), (1,)), ((), ()))
 TN = (((0,), (0,)), ((), ()))
@@ -197,16 +197,19 @@
                       normed_all.at[2:4, me, 0:every], d)
 
     def parts_out(d):
-        return t_copy(1, part_out.at[lax.rem(me + d, shards), :, 0:classes],
-                      part_in.at[me, :, 0:classes], d)
-
-    def grad_out(d):
-        mine = grads.at[0, me, 0:every]
+        return t_copy(1, part_out.at[lax.rem(me + d, shards)], part_in.at[me], d)
+
+    def logits_out(d):
+        mine = grads.at[1, me, 0:every, 0:classes]
         return t_copy(2, mine, mine, d)
 
     def backs_out(d):
-        return t_copy(3, part_out.at[lax.rem(me + d, shards), :, 0:blk],
-                      part_in.at[me, :, 0:blk], d)
+        return t_copy(3, normed_all.at[4, lax.rem(me + d, shards), 0:every],
+                      normed_all.at[5, me, 0:every], d)
+
+    def counts_out(d):
+        mine = normed_all.at[6, me, 0:every, 0:128]
+        return t_copy(4, mine, mine, d)
 
     def split(value):
         hi = value.astype(bf16)
@@ -224,6 +227,7 @@
             hit = jnp.where(segs[m : m + 1, at : at + rows] + cands * m == slots, 1.0, 0.0)
             counts = counts + jnp.sum(hit, -1, keepdims=True)
             pool[k] = hit.astype(bf16)
+        normed_all[6, me, 0:every, 0:128] = jnp.broadcast_to(counts, (every, 128)).astype(bf16)
         for b in range(shards):
             sums = jnp.zeros((every, blk), f32)
             for k in range(chunks):
@@ -233,6 +237,8 @@
             normed_all[1, b, 0:every] = lo
         for d in range(1, shards):
             sums_out(d).start()
+        for d in range(1, shards):
+            counts_out(d).start()
         normed_all[2, me, 0:every] = normed_all[0, me, 0:every]
         normed_all[3, me, 0:every] = normed_all[1, me, 0:every]
         own_head.wait()
@@ -255,13 +261,13 @@
             y = lax.dot_general(both, weight[me, cols, :], NT, preferred_element_type=f32)
             y = (y[: shards * every] + y[shards * every :]).astype(bf16)
             part = part + jnp.dot(y, head[cols, :], preferred_element_type=f32)
-        part_out[:, :, 0:classes] = part.reshape(shards, every, classes)
+        part_out[...] = part.reshape(shards, every, classes)
         for d in range(1, shards):
             parts_out(d).start()
         part_in[me] = part_out[me]
         for d in range(1, shards):
             parts_out(d).wait_recv()
-        logits = (logits + jnp.sum(part_in[:, :, 0:classes], 0)) / counts
+        logits = (logits + jnp.sum(part_in[...], 0)) / counts
         lanes = lax.broadcasted_iota(jnp.int32, (cands, cands), 1)
         diagonal = lanes == lax.broadcasted_iota(jnp.int32, (cands, cands), 0)
         target = []
@@ -271,28 +277,31 @@
         target = jnp.concatenate(target, 0).astype(jnp.int32)
         target = lax.broadcasted_iota(jnp.int32, (every, classes), 1) == target
         dlogit = (jax.nn.sigmoid(logits) - jnp.where(target, 1.0, 0.0)).astype(bf16)
+        grads[1, me, 0:every, 0:classes] = dlogit
+        for d in range(1, shards):
+            logits_out(d).start()
+        for d in range(1, shards):
+            counts_out(d).wait_recv()
+        for d in range(1, shards):
+            logits_out(d).wait_recv()
+        all_counts = flat(normed_all[6, :, 0:every, 0:128])[:, 0:1].astype(f32)
+        all_dlogit = flat(grads[1, :, 0:every, 0:classes])
         for b in range(4):
             cols = slice(b * quarter, (b + 1) * quarter)
-            dpool = lax.dot_general(dlogit, head[cols, :], NT, preferred_element_type=f32)
-            grads[0, me, 0:every, cols] = (dpool / counts).astype(bf16)
-        for d in range(1, shards):
-            grad_out(d).start()
-        for d in range(1, shards):
-            grad_out(d).wait_recv()
-        for d in range(1, shards):
-            parts_out(d).wait_send()
-        part_out[:, :, 0:blk] = jnp.dot(
-            flat(grads[0, :, 0:every]), weight[me], preferred_element_type=f32
-        ).reshape(shards, every, blk)
+            dpool = lax.dot_general(all_dlogit, head[cols, :], NT, preferred_element_type=f32)
+            grads[0, :, 0:every, cols] = (
+                (dpool / all_counts).astype(bf16).reshape(shards, every, quarter)
+            )
+        normed_all[4, :, 0:every] = (
+            jnp.dot(flat(grads[0, :, 0:every]), weight[me], preferred_element_type=f32)
+            .astype(bf16)
+            .reshape(shards, every, blk)
+        )
         for d in range(1, shards):
             backs_out(d).start()
-        part_in[me] = part_out[me]
+        normed_all[5, me, 0:every] = normed_all[4, me, 0:every]
         for d in range(1, shards):
             backs_out(d).wait_recv()
-        for b in range(shards):
-            hi, lo = split(part_in[b, :, 0:blk])
-            normed_all[4, b, 0:every] = hi
-            normed_all[5, b, 0:every] = lo
 
     def c_copy(k):
         return remote(din.at[k], grads.at[k, me], c_send.at[k], c_recv.at[k], (sec - 1, me))
@@ -318,7 +327,7 @@
             rhs = grads[k, :, :, cols].reshape(shards * rows, width // 4)
             total[:, cols] += lax.dot_general(lhs, rhs, TN, preferred_element_type=f32)
 
-    lag = jnp.clip(1 + 2 * (sec - (top - 4)), 1, chunks)
+    lag = jnp.where(sec == 0, 1, jnp.clip(1 + 2 * (sec - (top - 4)), 3, chunks))
 
     def columns_here():
         for d in range(1, shards):
@@ -351,7 +360,7 @@
 
         section_back(
             k,
-            lambda b: pick(normed_all[4, b, 0:every]) + pick(normed_all[5, b, 0:every]),
+            lambda b: pick(normed_all[5, b, 0:every]),
             lambda cols: pick(grads[0, me, 0:every, cols]),
         )
         return carry
@@ -440,7 +449,9 @@
     def _():
         for d in range(1, shards):
             sums_out(d).wait_send()
-            grad_out(d).wait_send()
+            counts_out(d).wait_send()
+            parts_out(d).wait_send()
+            logits_out(d).wait_send()
             backs_out(d).wait_send()
 
     @pl.when(sec < top)
@@ -525,8 +536,8 @@
             pltpu.VMEM((1, width), f32),
             pltpu.VMEM((shards, 1, width), f32),
             pltpu.VMEM((chunks, every, CHUNK), bf16),
-            pltpu.VMEM((shards, every, max(classes, blk)), f32),
-            pltpu.VMEM((shards, every, max(classes, blk)), f32),
+            pltpu.VMEM((shards, every, classes), f32),
+            pltpu.VMEM((shards, every, classes), f32),
             pltpu.VMEM((LENT, width // PIECES if chips == 2 else 16, blk), bf16),
             pltpu.VMEM((LENT, width // PIECES if chips == 2 else 16, blk), bf16),
             dma((3,)),
@@ -540,8 +551,8 @@
             dma((chunks, 2 * chips - 1)),
             dma((shards - 1,)),
             dma((shards - 1,)),
-            dma((4, shards - 1)),
-            dma((4, shards - 1)),
+            dma((5, shards - 1)),
+            dma((5, shards - 1)),
             dma((3, LENT)),
             dma((3, LENT)),
         ],

time: 178 us -> 170 us (0.955)
  Pallas kernels: 168 us -> 160 us
    pallas_call x1, Pallas kernels: 168 us -> 160 us  [per_device(): pl.pallas_call(functools.partial(kernel, sections, shards, chunks), out_s...]
where the time goes in v4:
time: 170 us
  Pallas kernels  160 us (94%)
  local copies, waits for them, and re-layouts  9.36 us (6%)
    pallas_call x1, Pallas kernels, per_device(): pl.pallas_call(functools.partial(kernel, sections, shards, chunks), out_s...  160 us
    unnamed x8, local copies, waits for them, and re-layouts  9.36 us

profile of v4, /device:TPU:0, one launch (start us, length us, event | category | flops | bytes accessed | tf_op | source)
XLA Modules:
  0.0 169.8 jit_solution(15575176979649909391)
XLA Ops:
  0.6 3.9 %copy.9 = bf16[1,512,2048]{1,2,0:T(8,128)(2,1)} copy(bf16[1,512,2048]{2,1,0:T(8,128)(2,1)} %param.8) | data formatting | bytes 4194304 | tf_op args[2]
  4.6 159.8 %shard_map.85 = (bf16[9,64,2048]{2,1,0:T(8,128)(2,1)}, bf16[512,2048]{1,0:T(8,128)(2,1)}, f32[1,2048]{1,0:T(1,128)}) custom-call(bf16[9,64,2048]{2,1,0:T(8,128)(2,1)} %bitcast.9, f32[1,2048]{1,0:T(1,128)} %gain.1, bf16[2048,512]{1,0:T(8,128)(2,1)} %bitcast.8, bf16[2048,512]{1,0:T(8,128)(2,1)} %head_hbm.1, s32[3,192]{1,0:T(4,128)} %segs.1, s32[3,16]{1,0:T(4,128)} %labels.1), custom_call_target="tpu_custom_call" | custom-call | flops 9663676416 | bytes 67108864 | tf_op jit(solution)/shard_map/pallas_call | solution.py:517
  164.4 0.0 copy-start
  164.4 3.5 %copy.13 = bf16[1,576,2048]{2,1,0:T(8,128)(2,1)} copy(bf16[1,576,2048]{2,1,0:T(8,128)(2,1)} %bitcast.6) | data formatting | bytes 4718592
  167.9 0.0 copy-done
  167.9 0.0 copy-start.1
  167.9 1.3 copy.14
  169.2 0.0 copy-done.1
  169.2 0.6 copy.15
Async XLA Ops:
  164.4 3.5 %copy-start = (bf16[512,2048]{1,0:T(8,128)(2,1)S(1)}, bf16[512,2048]{1,0:T(8,128)(2,1)}, u32[]{:S(2)}) copy-start(bf16[512,2048]{1,0:T(8,128)(2,1)} %get-tuple-element.7) | copy-start | bytes 6291460
  167.9 1.3 copy-start.1

commit v5 on v4

--- a/solution.py
+++ b/solution.py
@@ -9,7 +9,7 @@
 
 norm_eps = 1e-06
 MESH = pl.DeviceIdType.MESH
-CHUNK = 64
+CHUNK = 48
 PIECES = 16
 LENT = 5
 bf16, f32 = jnp.bfloat16, jnp.float32
@@ -317,7 +317,7 @@
             g_copy(k, 1, d, behind(d), ahead(d)).wait_recv()
             g_copy(k, 2, d, behind(d), pair).start()
 
-    def accumulate(k):
+    def accumulate(k, last=False):
         g_copy(k, 0, 0, pair, pair).wait_recv()
         for d in range(1, chips):
             g_copy(k, 2, d, behind(d, False), pair).wait_recv()
@@ -325,9 +325,13 @@
         for b in range(4):
             cols = slice(b * (width // 4), (b + 1) * (width // 4))
             rhs = grads[k, :, :, cols].reshape(shards * rows, width // 4)
-            total[:, cols] += lax.dot_general(lhs, rhs, TN, preferred_element_type=f32)
-
-    lag = jnp.where(sec == 0, 1, jnp.clip(1 + 2 * (sec - (top - 4)), 3, chunks))
+            term = lax.dot_general(lhs, rhs, TN, preferred_element_type=f32)
+            if last:
+                dproj[:, cols] = (total[:, cols] + term).astype(bf16)
+            else:
+                total[:, cols] += term
+
+    lag = jnp.where(sec == 0, 1, jnp.clip(2 + 3 * (sec - (top - 4)), 4, chunks - 1))
 
     def columns_here():
         for d in range(1, shards):
@@ -417,25 +421,21 @@
                 total[:, cols] += lax.dot_general(
                     sums, every_grad[:, cols], TN, preferred_element_type=f32
                 )
-
-    def relay_step(k, carry):
+        dproj[...] = total[...].astype(bf16)
+
+    def catch_up(k, carry):
+        accumulate(k - 1)
         relay(k)
         return carry
 
-    def accumulate_step(k, carry):
-        accumulate(k)
-        return carry
-
     @pl.when(sec < top)
     def _():
         @pl.when(lag + 1 >= chunks)
         def _():
             columns_here()
 
-        lax.fori_loop(chunks - lag, chunks, relay_step, 0)
-        lax.fori_loop(jnp.maximum(chunks - lag - 1, 0), chunks, accumulate_step, 0)
-
-    dproj[...] = total[...].astype(bf16)
+        lax.fori_loop(chunks - lag, chunks, catch_up, 0)
+        accumulate(chunks - 1, last=True)
 
     gain_all[me] = gain_acc[...]
     for d in range(1, shards):

time: 170 us -> 168 us (0.988)
  Pallas kernels: 160 us -> 158 us
    pallas_call x1, Pallas kernels: 160 us -> 158 us  [per_device(): pl.pallas_call(functools.partial(kernel, sections, shards, chunks), out_s...]
where the time goes in v5:
time: 168 us
  Pallas kernels  158 us (94%)
  local copies, waits for them, and re-layouts  9.36 us (6%)
    pallas_call x1, Pallas kernels, per_device(): pl.pallas_call(functools.partial(kernel, sections, shards, chunks), out_s...  158 us
    unnamed x8, local copies, waits for them, and re-layouts  9.36 us

profile of v5, /device:TPU:0, one launch (start us, length us, event | category | flops | bytes accessed | tf_op | source)
XLA Modules:
  0.0 168.0 jit_solution(6654973887488636024)
XLA Ops:
  0.6 3.9 %copy.9 = bf16[1,512,2048]{1,2,0:T(8,128)(2,1)} copy(bf16[1,512,2048]{2,1,0:T(8,128)(2,1)} %param.8) | data formatting | bytes 4194304 | tf_op args[2]
  4.6 157.9 %shard_map.85 = (bf16[12,48,2048]{2,1,0:T(8,128)(2,1)}, bf16[512,2048]{1,0:T(8,128)(2,1)}, f32[1,2048]{1,0:T(1,128)}) custom-call(bf16[12,48,2048]{2,1,0:T(8,128)(2,1)} %bitcast.9, f32[1,2048]{1,0:T(1,128)} %gain.1, bf16[2048,512]{1,0:T(8,128)(2,1)} %bitcast.8, bf16[2048,512]{1,0:T(8,128)(2,1)} %head_hbm.1, s32[3,192]{1,0:T(4,128)} %segs.1, s32[3,16]{1,0:T(4,128)} %labels.1), custom_call_target="tpu_custom_call" | custom-call | flops 9663676416 | bytes 67108864 | tf_op jit(solution)/shard_map/pallas_call | solution.py:517
  162.5 0.0 copy-start
  162.5 3.5 %copy.13 = bf16[1,576,2048]{2,1,0:T(8,128)(2,1)} copy(bf16[1,576,2048]{2,1,0:T(8,128)(2,1)} %bitcast.6) | data formatting | bytes 4718592
  166.0 0.0 copy-done
  166.0 0.0 copy-start.1
  166.0 1.3 copy.14
  167.4 0.0 copy-done.1
  167.4 0.6 copy.15
Async XLA Ops:
  162.5 3.5 %copy-start = (bf16[512,2048]{1,0:T(8,128)(2,1)S(1)}, bf16[512,2048]{1,0:T(8,128)(2,1)}, u32[]{:S(2)}) copy-start(bf16[512,2048]{1,0:T(8,128)(2,1)} %get-tuple-element.7) | copy-start | bytes 6291460
  166.0 1.3 copy-start.1

commit v6 on v5

--- a/solution.py
+++ b/solution.py
@@ -11,7 +11,7 @@
 MESH = pl.DeviceIdType.MESH
 CHUNK = 48
 PIECES = 16
-LENT = 5
+LENT = 3
 bf16, f32 = jnp.bfloat16, jnp.float32
 NT = (((1,), (1,)), ((), ()))
 TN = (((0,), (0,)), ((), ()))

time: 168 us -> 163 us (0.970)
  Pallas kernels: 158 us -> 153 us
    pallas_call x1, Pallas kernels: 158 us -> 153 us  [per_device(): pl.pallas_call(functools.partial(kernel, sections, shards, chunks), out_s...]
where the time goes in v6:
time: 163 us
  Pallas kernels  153 us (94%)
  local copies, waits for them, and re-layouts  9.36 us (6%)
    pallas_call x1, Pallas kernels, per_device(): pl.pallas_call(functools.partial(kernel, sections, shards, chunks), out_s...  153 us
    unnamed x8, local copies, waits for them, and re-layouts  9.36 us

profile of v6, /device:TPU:0, one launch (start us, length us, event | category | flops | bytes accessed | tf_op | source)
XLA Modules:
  0.0 162.9 jit_solution(9268997160441963620)
XLA Ops:
  0.6 3.9 %copy.9 = bf16[1,512,2048]{1,2,0:T(8,128)(2,1)} copy(bf16[1,512,2048]{2,1,0:T(8,128)(2,1)} %param.8) | data formatting | bytes 4194304 | tf_op args[2]
  4.6 152.9 %shard_map.85 = (bf16[12,48,2048]{2,1,0:T(8,128)(2,1)}, bf16[512,2048]{1,0:T(8,128)(2,1)}, f32[1,2048]{1,0:T(1,128)}) custom-call(bf16[12,48,2048]{2,1,0:T(8,128)(2,1)} %bitcast.9, f32[1,2048]{1,0:T(1,128)} %gain.1, bf16[2048,512]{1,0:T(8,128)(2,1)} %bitcast.8, bf16[2048,512]{1,0:T(8,128)(2,1)} %head_hbm.1, s32[3,192]{1,0:T(4,128)} %segs.1, s32[3,16]{1,0:T(4,128)} %labels.1), custom_call_target="tpu_custom_call" | custom-call | flops 9663676416 | bytes 67108864 | tf_op jit(solution)/shard_map/pallas_call | solution.py:517
  157.4 0.0 copy-start
  157.4 3.5 %copy.13 = bf16[1,576,2048]{2,1,0:T(8,128)(2,1)} copy(bf16[1,576,2048]{2,1,0:T(8,128)(2,1)} %bitcast.6) | data formatting | bytes 4718592
  161.0 0.0 copy-done
  161.0 0.0 copy-start.1
  161.0 1.3 copy.14
  162.3 0.0 copy-done.1
  162.3 0.6 copy.15
Async XLA Ops:
  157.4 3.5 %copy-start = (bf16[512,2048]{1,0:T(8,128)(2,1)S(1)}, bf16[512,2048]{1,0:T(8,128)(2,1)}, u32[]{:S(2)}) copy-start(bf16[512,2048]{1,0:T(8,128)(2,1)} %get-tuple-element.7) | copy-start | bytes 6291460
  161.0 1.3 copy-start.1
